TPU v7x, 1024 devices: a whole 4x4x32 slice. The times are simulated.
1024 devices in a mesh: section: 8 (over x_hi, y), expert: 32 (over z), copy: 4 (over x_lo, core).
Axes of the slice: x: 4 (x_hi: 2, x_lo: 2; x = x_hi * 2 + x_lo), y: 4, z: 32, core: 2. Of those that a mesh axis runs over, the one named last changes fastest.
Arguments:
- pending: bfloat16 [8, 4096, 4096], P('section', 'expert', 'copy'), may hold values from -6 to 6
- hidden: bfloat16 [8, 4096, 768], P('section', 'expert'), may hold values from -6 to 6
- logits: float32 [8, 4096, 4], P('section', 'expert')
- routes: int32 [8, 4096, 1], P('section', 'expert'), may hold values from 0 to 3; in each aligned block of 128 rows (0 to 127, 128 to 255, ..., all dimensions but the last counted through in order) at most 36 rows name the same one
- router_weight: float32 [8, 4096, 4], P('section', 'copy'), may hold values from -1.5 to 1.5
- down_weight: bfloat16 [8, 4, 768, 4096], P('section', 'copy', None, 'expert'), may hold values from -0.21875 to 0.21875
- master: float32 [8, 4, 768, 4096], P('section', 'copy', None, 'expert'), may hold values from -0.21875 to 0.21875
- moment_first: float32 [8, 4, 768, 4096], P('section', 'copy', None, 'expert'), may hold values from -64 to 64
- moment_second: float32 [8, 4, 768, 4096], P('section', 'copy', None, 'expert'), may hold values from 10 to 341
- push_plan: int32 [8, 4, 32, 96, 1], P('section', 'copy', 'expert'), may hold values from 0 to 31; in each aligned block of 96 rows (0 to 95, 96 to 191, ..., all dimensions but the last counted through in order) at most 5 rows name the same one
Outputs:
- input_grads: bfloat16 [8, 4096, 4096], P('section', 'expert', 'copy')
- master_out: float32 [8, 4, 768, 4096], P('section', 'copy', None, 'expert')
- moment_first_out: float32 [8, 4, 768, 4096], P('section', 'copy', None, 'expert')
- moment_second_out: float32 [8, 4, 768, 4096], P('section', 'copy', None, 'expert')
- serving: bfloat16 [8, 4, 32, 160, 8, 128], P('section', 'copy', 'expert')
Inputs may be any that keep to these rules, and one draw needn't show every extreme that they name: `routes`: among the tokens of one index of expert, at most 36 are routed to any one expert. `push_plan`: among the blocks of one device, at most 5 go to any one owner.
All inputs are finite; a program needn't handle non-finite values.
Results may differ from a plain program's by a relative error of at most 0.0013.
Values may be sent and summed in bfloat16 or wider, within the bound.
A program may use at most 32 MiB of HBM per device.

v0:
```python
import jax
import jax.numpy as jnp
from jax import lax
from jax.sharding import PartitionSpec as P

PUSH_ROWS = 8


beta_first = 0.9
beta_second = 0.95
learn_rate = 0.002
decay_rate = 0.1
adam_eps = 1e-08
bias_first = 1.0 - 0.9**10
bias_second = 1.0 - 0.95**10


def passed_along(shard, axis, by):
    devices = lax.axis_size(axis)
    return lax.ppermute(shard, axis, [(i, (i + by) % devices) for i in range(devices)])


def per_device(
    pending,
    hidden,
    logits,
    routes,
    router_weight,
    down_weight,
    master,
    moment_first,
    moment_second,
    push_plan,
):
    incoming = passed_along(pending, "section", -1)[0]
    hidden_rows = hidden[0]
    logit_rows = logits[0]
    route_ids = routes[0, :, 0]
    tok_rows, width = incoming.shape
    n_experts = logit_rows.shape[1]
    groups = lax.axis_size("expert")
    split_ways = groups // n_experts
    piece_width = width // split_ways
    ff_win = hidden_rows.shape[1]
    capacity = tok_rows * 9 // (n_experts * 8)
    probability = jax.nn.softmax(logit_rows, axis=-1)
    expert_ids = lax.broadcasted_iota(jnp.int32, (tok_rows, n_experts), 1)
    onehot_int = (route_ids[:, None] == expert_ids).astype(jnp.int32)
    onehot = onehot_int.astype(jnp.float32)
    gate_value = jnp.sum(probability * onehot, axis=-1)
    gate_half = gate_value.astype(jnp.bfloat16)
    running = jnp.cumsum(onehot_int, axis=0)
    rank_ids = jnp.sum(running * onehot_int, axis=1) - 1
    slot_expert = lax.broadcasted_iota(jnp.int32, (n_experts, capacity, tok_rows), 0)
    slot_rank = lax.broadcasted_iota(jnp.int32, (n_experts, capacity, tok_rows), 1)
    placing = (
        (route_ids[None, None, :] == slot_expert) & (rank_ids[None, None, :] == slot_rank)
    ).astype(jnp.bfloat16)
    send_rows = jnp.einsum(
        "ect,tjd->ejcd",
        placing,
        incoming.reshape(tok_rows, split_ways, piece_width),
        preferred_element_type=jnp.float32,
    )
    send_rows = send_rows.astype(jnp.bfloat16).reshape(groups, capacity, piece_width)
    send_hidden = jnp.einsum(
        "ect,tf->ecf", placing, hidden_rows, preferred_element_type=jnp.float32
    ).astype(jnp.bfloat16)
    send_hidden = jnp.broadcast_to(
        send_hidden[:, None], (n_experts, split_ways, capacity, ff_win)
    ).reshape(groups, capacity, ff_win)
    send_gate = jnp.einsum(
        "ect,t->ec", placing, gate_half, preferred_element_type=jnp.float32
    ).astype(jnp.bfloat16)
    send_gate = jnp.broadcast_to(send_gate[:, None], (n_experts, split_ways, capacity)).reshape(
        groups, capacity
    )
    weight_piece = down_weight[0, 0]
    row_data, hid_data, gate_data = (
        lax.all_to_all(send_rows, "expert", split_axis=0, concat_axis=0, tiled=True),
        lax.all_to_all(send_hidden, "expert", split_axis=0, concat_axis=0, tiled=True),
        lax.all_to_all(send_gate, "expert", split_axis=0, concat_axis=0, tiled=True),
    )
    outputs = jnp.einsum("sif,fd->sid", hid_data, weight_piece, preferred_element_type=jnp.float32)
    partial_value = jnp.sum(outputs * row_data.astype(jnp.float32), axis=2)
    scaled = (gate_data.astype(jnp.float32)[:, :, None] * row_data.astype(jnp.float32)).astype(
        jnp.bfloat16
    )
    partial_value, scaled = (partial_value, scaled)
    returned = lax.all_to_all(partial_value, "expert", split_axis=0, concat_axis=0, tiled=True)
    summed = jnp.sum(returned.reshape(n_experts, split_ways, capacity), axis=1)
    gate_local = jnp.einsum(
        "ect,ec->t", placing.astype(jnp.float32), summed, precision=lax.Precision.HIGHEST
    )
    gate_grad = lax.psum(gate_local, "copy")
    logit_grad = (gate_grad * gate_value)[:, None] * (onehot - probability)
    router_term = jnp.einsum(
        "te,de->td", logit_grad, router_weight[0], precision=lax.Precision.HIGHEST
    )
    input_grad = (incoming.astype(jnp.float32) + router_term).astype(jnp.bfloat16)
    gradient = jnp.einsum("sif,sid->fd", hid_data, scaled, preferred_element_type=jnp.float32)
    first_moment = beta_first * moment_first[0, 0] + (1.0 - beta_first) * gradient
    second_moment = beta_second * moment_second[0, 0] + (1.0 - beta_second) * gradient * gradient
    update = (
        first_moment / bias_first / (jnp.sqrt(second_moment / bias_second) + adam_eps)
        + decay_rate * master[0, 0]
    )
    fresh_master = master[0, 0] - learn_rate * update
    ff_rows = fresh_master.shape[0]
    block_count = ff_rows // PUSH_ROWS
    slot_most = max(2, (3 * block_count + 2 * groups - 1) // (2 * groups))
    blocks = fresh_master.astype(jnp.bfloat16).reshape(block_count, PUSH_ROWS, piece_width)
    plan_ids = push_plan[0, 0, 0, :, 0]
    owner_ids = lax.broadcasted_iota(jnp.int32, (block_count, groups), 1)
    owner_hot = (plan_ids[:, None] == owner_ids).astype(jnp.int32)
    earlier = jnp.cumsum(owner_hot, axis=0) - owner_hot
    block_rank = jnp.sum(earlier * owner_hot, axis=1)
    target_owner = lax.broadcasted_iota(jnp.int32, (groups, slot_most, block_count), 0)
    target_slot = lax.broadcasted_iota(jnp.int32, (groups, slot_most, block_count), 1)
    sending = (
        (plan_ids[None, None, :] == target_owner) & (block_rank[None, None, :] == target_slot)
    ).astype(jnp.bfloat16)
    outgoing = jnp.einsum(
        "omb,brd->omrd", sending, blocks, preferred_element_type=jnp.float32
    ).astype(jnp.bfloat16)
    arrived = lax.all_to_all(outgoing, "expert", split_axis=0, concat_axis=0, tiled=True)
    arrived = arrived.reshape(groups * slot_most, PUSH_ROWS, piece_width)
    return (
        input_grad[None],
        fresh_master[None, None],
        first_moment[None, None],
        second_moment[None, None],
        arrived[None, None, None],
    )


def solution(mesh):
    return jax.shard_map(
        per_device,
        mesh=mesh,
        in_specs=(
            P("section", "expert", "copy"),
            P("section", "expert", None),
            P("section", "expert", None),
            P("section", "expert", None),
            P("section", "copy", None),
            P("section", "copy", None, "expert"),
            P("section", "copy", None, "expert"),
            P("section", "copy", None, "expert"),
            P("section", "copy", None, "expert"),
            P("section", "copy", "expert", None, None),
        ),
        out_specs=(
            P("section", "expert", "copy"),
            P("section", "copy", None, "expert"),
            P("section", "copy", None, "expert"),
            P("section", "copy", None, "expert"),
            P("section", "copy", "expert", None, None, None),
        ),
        check_vma=False,
    )
```

profile of v0, /device:TPU:24, one launch (start us, length us, event | category | flops | bytes accessed | tf_op | source)
XLA Modules:
  0.0 379.6 jit_solution(1294531176010207246)
XLA Ops:
  0.7 2.8 collective-permute-start
  3.4 0.8 copy.29
  4.2 0.7 reduce_max.9
  4.9 0.7 fusion.21
  5.7 0.2 reduce_window_sum.22
  5.9 0.8 select_reduce_fusion
  6.7 0.2 fusion.22
  6.9 0.9 multiply_reduce_fusion
  7.7 0.8 fusion.26
  8.6 0.6 copy.30
  9.2 28.7 %all-to-all-start.3 = ((bf16[32,1,36]{2,1,0:T(2,128)(2,1)}), bf16[32,1,36]{2,1,0:T(2,128)(2,1)S(1)}, u32[]{:S(2)}, u32[]{:S(2)}) async-start(bf16[32,1,36]{2,1,0:T(2,128)(2,1)} %copy.30), calls=%async_computation.3 | async-start | bytes 32768 | tf_op jit(solution)/shard_map/all_to_all | solution.py:82
  38.1 1.6 convolution_convert_fusion.1
  39.8 20.4 %all-to-all-done.3 = bf16[32,1,36]{2,1,0:T(2,128)(2,1)S(1)} async-done(((bf16[32,1,36]{2,1,0:T(2,128)(2,1)}), bf16[32,1,36]{2,1,0:T(2,128)(2,1)S(1)}, u32[]{:S(2)}, u32[]{:S(2)}) %all-to-all-start.3) | async-done | bytes 2336 | tf_op jit(solution)/shard_map/all_to_all | solution.py:82
  60.2 3.9 %all-to-all-start.1 = ((bf16[32,36,128]{2,1,0:T(8,128)(2,1)}), bf16[32,36,128]{2,1,0:T(8,128)(2,1)S(1)}, u32[]{:S(2)}, u32[]{:S(2)}) async-start(bf16[32,36,128]{2,1,0:T(8,128)(2,1)} %bitcast.12), calls=%async_computation.1 | async-start | bytes 655360 | tf_op jit(solution)/shard_map/all_to_all | solution.py:80
  64.1 0.2 convolution_convert_fusion.2
  64.3 46.8 %all-to-all-done.1 = bf16[32,36,128]{2,1,0:T(8,128)(2,1)S(1)} async-done(((bf16[32,36,128]{2,1,0:T(8,128)(2,1)}), bf16[32,36,128]{2,1,0:T(8,128)(2,1)S(1)}, u32[]{:S(2)}, u32[]{:S(2)}) %all-to-all-start.1) | async-done | bytes 294944 | tf_op jit(solution)/shard_map/all_to_all | solution.py:80
  111.1 1.4 broadcast_in_dim.12
  112.5 4.1 %all-to-all-start = ((bf16[32,36,768]{2,1,0:T(8,128)(2,1)}), bf16[32,36,768]{2,1,0:T(8,128)(2,1)S(1)}, u32[]{:S(2)}, u32[]{:S(2)}) async-start(bf16[32,36,768]{2,1,0:T(8,128)(2,1)} %bitcast.4), calls=%async_computation | async-start | bytes 3932160 | tf_op jit(solution)/shard_map/all_to_all | solution.py:81
  116.9 0.2 select_reduce_fusion.1
  117.1 185.7 %all-to-all-done = bf16[32,36,768]{2,1,0:T(8,128)(2,1)S(1)} async-done(((bf16[32,36,768]{2,1,0:T(8,128)(2,1)}), bf16[32,36,768]{2,1,0:T(8,128)(2,1)S(1)}, u32[]{:S(2)}, u32[]{:S(2)}) %all-to-all-start) | async-done | bytes 1769504 | tf_op jit(solution)/shard_map/all_to_all | solution.py:81
  302.8 1.4 fusion
  304.2 3.8 %all-to-all-start.2 = ((f32[32,1,36]{2,1,0:T(1,128)}), f32[32,1,36]{2,1,0:T(1,128)S(1)}, u32[]{:S(2)}, u32[]{:S(2)}) async-start(f32[32,1,36]{2,1,0:T(1,128)} %bitcast.13), calls=%async_computation.2 | async-start | bytes 32768 | tf_op jit(solution)/shard_map/all_to_all | solution.py:90
  308.1 3.2 convert_bitcast_fusion
  311.4 0.2 convolution_convert_fusion
  311.6 0.9 copy.32
  312.4 17.5 %all-to-all-done.2 = f32[32,1,36]{2,1,0:T(1,128)S(1)} async-done(((f32[32,1,36]{2,1,0:T(1,128)}), f32[32,1,36]{2,1,0:T(1,128)S(1)}, u32[]{:S(2)}, u32[]{:S(2)}) %all-to-all-start.2) | async-done | bytes 4640 | tf_op jit(solution)/shard_map/all_to_all | solution.py:90
  329.9 4.3 %all-to-all-start.4 = ((bf16[32,5,8,128]{3,2,1,0:T(8,128)(2,1)}), bf16[32,5,8,128]{3,2,1,0:T(8,128)(2,1)S(1)}, u32[]{:S(2)}, u32[]{:S(2)}) async-start(bf16[32,5,8,128]{3,2,1,0:T(8,128)(2,1)} %copy.32), calls=%async_computation.4 | async-start | bytes 655360 | tf_op jit(solution)/shard_map/all_to_all | solution.py:126
  334.2 0.2 convolution_bitcast_fusion.1
  334.4 5.7 %psum.7 = f32[128]{0:T(128)S(1)} all-reduce(f32[128]{0:T(128)S(1)} %convolution_bitcast_fusion.1), channel_id=1, replica_groups=mesh['section'=8,'expert'=32,'copy'=4] {'copy'}, use_global_device_ids=true, to_apply=%region_4.5 | all-reduce | flops 128 | bytes 1024 | tf_op jit(solution)/shard_map/psum | solution.py:95
  340.1 1.4 fusion.8
  341.5 37.4 %all-to-all-done.4 = bf16[32,5,8,128]{3,2,1,0:T(8,128)(2,1)S(1)} async-done(((bf16[32,5,8,128]{3,2,1,0:T(8,128)(2,1)}), bf16[32,5,8,128]{3,2,1,0:T(8,128)(2,1)S(1)}, u32[]{:S(2)}, u32[]{:S(2)}) %all-to-all-start.4) | async-done | bytes 327712 | tf_op jit(solution)/shard_map/all_to_all | solution.py:126
  378.9 0.7 copy.44
  (24 shorter events, 0.5 us)
Async XLA Ops:
  0.6 63.5 %copy-start = (bf16[1,128,768]{2,1,0:T(8,128)(2,1)S(1)}, bf16[1,128,768]{2,1,0:T(8,128)(2,1)}, u32[]{:S(2)}) copy-start(bf16[1,128,768]{2,1,0:T(8,128)(2,1)} %param.11) | copy-start | bytes 589828
  0.6 63.5 %copy-start.2 = (s32[1,128,1]{1,2,0:T(1,128)S(1)}, s32[1,128,1]{1,2,0:T(1,128)}, u32[]{:S(2)}) copy-start(s32[1,128,1]{1,2,0:T(1,128)} %param.13) | copy-start | bytes 1540
  0.7 37.3 %collective-permute-start = (bf16[1,128,1024]{2,1,0:T(8,128)(2,1)}, bf16[1,128,1024]{2,1,0:T(8,128)(2,1)S(1)}, u32[]{:S(2)}, u32[]{:S(2)}) collective-permute-start(bf16[1,128,1024]{2,1,0:T(8,128)(2,1)} %param.10), channel_id=1, source_target_pairs={{0,896},{128,0},{256,128},{384,256},{512,384},{640,512},{768,640},... | collective-permute-start | bytes 786440 | tf_op jit(solution)/shard_map/ppermute | solution.py:20
  9.2 51.0 %all-to-all-start.3 = ((bf16[32,1,36]{2,1,0:T(2,128)(2,1)}), bf16[32,1,36]{2,1,0:T(2,128)(2,1)S(1)}, u32[]{:S(2)}, u32[]{:S(2)}) async-start(bf16[32,1,36]{2,1,0:T(2,128)(2,1)} %copy.30), calls=%async_computation.3 | async-start | bytes 32768 | tf_op jit(solution)/shard_map/all_to_all | solution.py:82
  60.2 50.9 %all-to-all-start.1 = ((bf16[32,36,128]{2,1,0:T(8,128)(2,1)}), bf16[32,36,128]{2,1,0:T(8,128)(2,1)S(1)}, u32[]{:S(2)}, u32[]{:S(2)}) async-start(bf16[32,36,128]{2,1,0:T(8,128)(2,1)} %bitcast.12), calls=%async_computation.1 | async-start | bytes 655360 | tf_op jit(solution)/shard_map/all_to_all | solution.py:80
  112.5 4.2 %copy-start.4 = (s32[1,1,1,96,1]{3,4,2,1,0:T(1,128)S(1)}, s32[1,1,1,96,1]{3,4,2,1,0:T(1,128)}, u32[]{:S(2)}) copy-start(s32[1,1,1,96,1]{3,4,2,1,0:T(1,128)} %param.19) | copy-start | bytes 1156
  112.5 190.3 %copy-start.6 = (bf16[1,1,768,128]{3,2,1,0:T(8,128)(2,1)S(1)}, bf16[1,1,768,128]{3,2,1,0:T(8,128)(2,1)}, u32[]{:S(2)}) copy-start(bf16[1,1,768,128]{3,2,1,0:T(8,128)(2,1)} %param.15) | copy-start | bytes 589828
  112.5 190.3 %all-to-all-start = ((bf16[32,36,768]{2,1,0:T(8,128)(2,1)}), bf16[32,36,768]{2,1,0:T(8,128)(2,1)S(1)}, u32[]{:S(2)}, u32[]{:S(2)}) async-start(bf16[32,36,768]{2,1,0:T(8,128)(2,1)} %bitcast.4), calls=%async_computation | async-start | bytes 3932160 | tf_op jit(solution)/shard_map/all_to_all | solution.py:81
  116.6 191.4 %copy-start.5 = (f32[1,1,768,128]{3,2,1,0:T(8,128)S(1)}, f32[1,1,768,128]{3,2,1,0:T(8,128)}, u32[]{:S(2)}) copy-start(f32[1,1,768,128]{3,2,1,0:T(8,128)} %param.18) | copy-start | bytes 1179652
  304.2 25.7 %all-to-all-start.2 = ((f32[32,1,36]{2,1,0:T(1,128)}), f32[32,1,36]{2,1,0:T(1,128)S(1)}, u32[]{:S(2)}, u32[]{:S(2)}) async-start(f32[32,1,36]{2,1,0:T(1,128)} %bitcast.13), calls=%async_computation.2 | async-start | bytes 32768 | tf_op jit(solution)/shard_map/all_to_all | solution.py:90
  308.1 32.0 %copy-start.1 = (f32[1,128,4]{1,2,0:T(4,128)S(1)}, f32[1,128,4]{1,2,0:T(4,128)}, u32[]{:S(2)}) copy-start(f32[1,128,4]{1,2,0:T(4,128)} %param.12) | copy-start | bytes 6148
  308.1 32.0 %copy-start.3 = (f32[1,1024,4]{1,2,0:T(4,128)S(1)}, f32[1,1024,4]{1,2,0:T(4,128)}, u32[]{:S(2)}) copy-start(f32[1,1024,4]{1,2,0:T(4,128)} %param.14) | copy-start | bytes 49156
  329.9 49.0 %all-to-all-start.4 = ((bf16[32,5,8,128]{3,2,1,0:T(8,128)(2,1)}), bf16[32,5,8,128]{3,2,1,0:T(8,128)(2,1)S(1)}, u32[]{:S(2)}, u32[]{:S(2)}) async-start(bf16[32,5,8,128]{3,2,1,0:T(8,128)(2,1)} %copy.32), calls=%async_computation.4 | async-start | bytes 655360 | tf_op jit(solution)/shard_map/all_to_all | solution.py:126
where the time goes:
time: 384 us; the launch traced here: 380 us
  waiting for transfers between devices  308 us (80%)
  starting transfers between devices  47.7 us (12%)
  matrix products  9.08 us (2%)
  blocking collectives  5.66 us (1%)
  local copies, waits for them, and re-layouts  4.64 us (1%)
  other arithmetic  3.92 us (1%)
    all_to_all x1, waiting for transfers between devices, per_device(): lax.all_to_all(send_hidden, 'expert', split_axis=0, concat_axis=0, tiled=...  186 us
    all_to_all x1, waiting for transfers between devices, per_device(): lax.all_to_all(send_rows, 'expert', split_axis=0, concat_axis=0, tiled=True)  46.8 us
    all_to_all x1, waiting for transfers between devices, per_device(): lax.all_to_all(outgoing, 'expert', split_axis=0, concat_axis=0, tiled=True)  37.4 us
    all_to_all x1, starting transfers between devices, per_device(): lax.all_to_all(send_gate, 'expert', split_axis=0, concat_axis=0, tiled=True)  28.7 us
    all_to_all x1, waiting for transfers between devices, per_device(): lax.all_to_all(send_gate, 'expert', split_axis=0, concat_axis=0, tiled=True)  20.4 us
    all_to_all x1, waiting for transfers between devices, per_device(): lax.all_to_all(partial_value, 'expert', split_axis=0, concat_axis=0, tile...  17.5 us
  transfers between devices with their start and end apart: 6, of which 5 were waited for; matrix products, arithmetic and copies ran while one was open for 4% of the time, Pallas kernels for 0%

commit v1 on v0

v1 whole, which is shorter than its diff:
```python
import functools

import jax
import jax.numpy as jnp
from jax import lax
from jax.experimental import pallas as pl
from jax.experimental.pallas import tpu as pltpu
from jax.sharding import PartitionSpec as P

PUSH_ROWS = 8
EXPERTS = 4
LANES = 128

beta_first = 0.9
beta_second = 0.95
learn_rate = 0.002
decay_rate = 0.1
adam_eps = 1e-08
bias_first = 1.0 - 0.9**10
bias_second = 1.0 - 0.95**10

F32 = jnp.float32
BF16 = jnp.bfloat16
I32 = jnp.int32
HIGHEST = lax.Precision.HIGHEST


def iota(shape, dim):
    return lax.broadcasted_iota(I32, shape, dim)


def mm(x, y, dims=((1,), (0,)), precision=None):
    return lax.dot_general(x, y, (dims, ((), ())), precision=precision, preferred_element_type=F32)


def kernel(
    n_sec, nz, slot_rows, gate_row,
    pend, hid, log_t, route_t, rw_t, w_hbm, ma_hbm, m1_hbm, m2_hbm, plan,
    ig_out, ma_out, m1_out, m2_out, serv,
    inc, hsend, hbuf, rsend, rbuf, scaled, gates, big, psend, ret_s, ret_r, cp_s, cp_r,
    wv, mav, m1v, m2v, fresh,
    ld_sem, st_sem, pend_sem, own_sem, ha_s, ha_r, zs, zr, xs, xr, cs, cr, rs, rr, ps, pr, gs, gr, ks, kr,
):
    grp = nz // EXPERTS
    cp = slot_rows
    tok = hid.shape[0]
    half = hid.shape[1] // 2
    ff = 2 * half
    s, z, c = lax.axis_index("section"), lax.axis_index("expert"), lax.axis_index("copy")
    a, b = c // 2, c % 2
    e, m = z // grp, z % grp
    here = (e // 2) * (2 * grp) + m * 2 + e % 2

    def place(p):
        q = p // grp
        return (q // 2) * (2 * grp) + (p % grp) * 2 + q % 2

    def remote(src, dst, send, recv, **axis):
        return pltpu.make_async_remote_copy(
            src_ref=src, dst_ref=dst, send_sem=send, recv_sem=recv,
            device_id=axis, device_id_type=pl.DeviceIdType.MESH,
        )

    loads = [
        pltpu.make_async_copy(src, dst, ld_sem.at[i])
        for i, (src, dst) in enumerate(((w_hbm, wv), (m1_hbm, m1v), (m2_hbm, m2v), (ma_hbm, mav)))
    ]
    for load in loads:
        load.start()

    barrier = pltpu.get_barrier_semaphore()
    prev_sec, next_sec = lax.rem(s + n_sec - 1, n_sec), lax.rem(s + 1, n_sec)

    def greet(**axis):
        pl.semaphore_signal(barrier, inc=1, device_id=axis, device_id_type=pl.DeviceIdType.MESH)

    greet(section=prev_sec)
    greet(section=next_sec)
    for k in range(1, 4):
        greet(copy=lax.rem(c + k, 4))

    @pl.loop(1, nz)
    def _(k):
        greet(expert=lax.rem(z + k, nz))

    pl.semaphore_wait(barrier, nz - 1 + 3 + 2)

    pend_copy = remote(pend, inc, pend_sem.at[0], pend_sem.at[1], section=prev_sec)
    pend_copy.start()

    logit = log_t[...]
    expd = jnp.exp(logit - jnp.max(logit, axis=0, keepdims=True))
    prob = expd / jnp.sum(expd, axis=0, keepdims=True)
    rid = route_t[...]
    onehot = (iota((EXPERTS, tok), 0) == rid).astype(F32)
    gate = jnp.sum(prob * onehot, axis=0, keepdims=True)
    hot8 = (iota((8, tok), 0) == rid).astype(F32)
    upper = (iota((tok, tok), 0) <= iota((tok, tok), 1)).astype(F32)
    running = mm(hot8.astype(BF16), upper.astype(BF16))
    rank = jnp.sum(running * hot8, axis=0, keepdims=True).astype(I32) - 1
    slot = rid * cp + rank
    placing = (iota((EXPERTS * cp, tok), 0) == slot).astype(F32).astype(BF16)
    gate8 = jnp.broadcast_to(gate, (8, tok)).astype(BF16)
    by_rank = []
    for x in range(EXPERTS):
        rank_x = jnp.where(rid == x, rank, -1)
        by_rank.append((iota((LANES, tok), 0) == rank_x).astype(F32))

    packed = mm(placing, hid[...]).astype(BF16)
    for x in range(EXPERTS):
        for h in range(2):
            hsend[h, x] = packed[x * cp:(x + 1) * cp, h * half:(h + 1) * half]

    def first_copy(d):
        other = lax.rem(e + d, EXPERTS)
        return remote(hsend.at[a, other], hbuf.at[a, b, m, e % 2], ha_s.at[d], ha_r.at[e % 2],
                      expert=other * grp + m)

    own_hidden = pltpu.make_async_copy(hsend.at[a, e], hbuf.at[a, b, m, e % 2], own_sem.at[0])

    @pl.when(b == e // 2)
    def _():
        for d in range(1, EXPERTS):
            first_copy(d).start()
        own_hidden.start()

    gate_rows = [
        mm(gate8, by_rank[x].astype(BF16), ((1,), (1,)))[0:1] for x in range(EXPERTS)
    ]

    pend_copy.wait_recv()
    for x in range(EXPERTS):
        rows = mm(placing[x * cp:(x + 1) * cp], inc[...])
        rid_rows = iota((cp, LANES), 0)
        for j in range(grp):
            piece = rows[:, j * LANES:(j + 1) * LANES]
            rsend[x * grp + j] = jnp.where(rid_rows >= gate_row, gate_rows[x], piece).astype(BF16)

    def row_copy(k):
        dest = lax.rem(z + k, nz)
        return remote(rsend.at[dest], rbuf.at[here], rs.at[k], rr.at[here], expert=dest)

    def row_arrival(k):
        src = lax.rem(z + k, nz)
        return remote(rsend.at[src], rbuf.at[place(src)], rs.at[k], rr.at[place(src)], expert=src)

    @pl.loop(1, nz // 2 + 1)
    def _(k):
        row_copy(k).start()

        @pl.when(k < nz // 2)
        def _():
            row_copy(nz - k).start()

    own_rows = pltpu.make_async_copy(rsend.at[z], rbuf.at[here], own_sem.at[1])
    own_rows.start()

    def chain_copy(block, way):
        return remote(hbuf.at[a, b, block], hbuf.at[a, b, block], zs.at[way, block], zr.at[block],
                      expert=lax.rem(z + (1 if way == 0 else nz - 1), nz))

    def x_copy(block, h):
        return remote(hbuf.at[h, b, block], hbuf.at[h, b, block], xs.at[block], xr.at[block],
                      copy=(1 - a) * 2 + b)

    def core_copy(block, h, kind, core):
        return remote(hbuf.at[h, core, block], hbuf.at[h, core, block], cs.at[kind, block],
                      cr.at[kind, block], copy=a * 2 + 1 - b)

    for i in range(2):
        @pl.when(2 * b + i != e)
        def _():
            remote(hsend.at[a, 0], hbuf.at[a, b, m, i], ha_s.at[0], ha_r.at[i], expert=m).wait_recv()

    @pl.when(b == e // 2)
    def _():
        own_hidden.wait()

    def spread(block):
        x_copy(block, a).start()
        core_copy(block, a, 0, b).start()

    @pl.when(m < grp - 1)
    def _():
        chain_copy(m, 0).start()

    @pl.when(m > 0)
    def _():
        chain_copy(m, 1).start()

    spread(m)

    @pl.loop(1, grp)
    def _(k):
        @pl.when(m - k >= 0)
        def _():
            chain_copy(m - k, 0).wait_recv()

            @pl.when(m < grp - 1)
            def _():
                chain_copy(m - k, 0).start()

            spread(m - k)

        @pl.when(m + k < grp)
        def _():
            chain_copy(m + k, 1).wait_recv()

            @pl.when(m > 0)
            def _():
                chain_copy(m + k, 1).start()

            spread(m + k)

    @pl.loop(0, grp)
    def _(block):
        x_copy(block, 1 - a).wait_recv()
        core_copy(block, 1 - a, 1, b).start()

    n_blocks = plan.shape[1]
    most = psend.shape[1] // PUSH_ROWS
    owner = plan[...]
    owner_hot = (iota((nz, n_blocks), 0) == owner).astype(F32)
    before = (iota((n_blocks, n_blocks), 0) < iota((n_blocks, n_blocks), 1)).astype(F32)
    earlier = mm(owner_hot.astype(BF16), before.astype(BF16))
    block_rank = jnp.sum(earlier * owner_hot, axis=0, keepdims=True)
    block_slot = jnp.broadcast_to(owner.astype(F32) * most + block_rank, (8, n_blocks))
    widen = (iota((n_blocks, ff), 1) // PUSH_ROWS == iota((n_blocks, ff), 0)).astype(F32)
    key = mm(block_slot.astype(BF16), widen.astype(BF16))[0:1].astype(I32)
    key = key * PUSH_ROWS + iota((1, ff), 1) % PUSH_ROWS
    big[...] = (iota((nz * most * PUSH_ROWS, ff), 0) == key).astype(F32).astype(BF16)

    for load in loads:
        load.wait()

    @pl.loop(0, grp)
    def _(block):
        core_copy(block, a, 0, 1 - b).wait_recv()
        core_copy(block, 1 - a, 1, 1 - b).wait_recv()

    own_rows.wait()

    @pl.loop(1, nz)
    def _(k):
        row_arrival(k).wait_recv()

    gates[...] = jnp.zeros(gates.shape, F32)
    for p in range(nz):
        gates[p:p + 1, :] = rbuf[p, 32:48, :].astype(F32)[gate_row - 32:gate_row - 31]
    gate_cols = gates[...].T
    for p in range(nz):
        scaled[p] = (gate_cols[0:cp, p:p + 1] * rbuf[p].astype(F32)).astype(BF16)
    scaled_all = scaled[...].reshape(nz * cp, LANES)
    for h in range(2):
        hidden_h = hbuf[h].reshape(nz * cp, half)
        grad = mm(scaled_all, hidden_h, ((0,), (0,))).T
        rows_h = pl.ds(h * half, half)
        first = beta_first * m1v[rows_h, :] + (1.0 - beta_first) * grad
        second = beta_second * m2v[rows_h, :] + (1.0 - beta_second) * grad * grad
        update = first / bias_first / (jnp.sqrt(second / bias_second) + adam_eps) + decay_rate * mav[rows_h, :]
        new = mav[rows_h, :] - learn_rate * update
        m1v[rows_h, :] = first
        m2v[rows_h, :] = second
        mav[rows_h, :] = new
        fresh[rows_h, :] = new.astype(BF16)
    per_owner = most * PUSH_ROWS
    for x in range(EXPERTS):
        part = mm(big[x * grp * per_owner:(x + 1) * grp * per_owner, :], fresh[...])
        for j in range(grp):
            psend[x * grp + j] = part[j * per_owner:(j + 1) * per_owner].astype(BF16)

    def push_copy(k):
        dest = lax.rem(z + k, nz)
        return remote(psend.at[dest], serv.at[z], ps.at[k], pr.at[z], expert=dest)

    def push_arrival(k):
        src = lax.rem(z + k, nz)
        return remote(psend.at[src], serv.at[src], ps.at[k], pr.at[src], expert=src)

    @pl.loop(1, nz // 2 + 1)
    def _(k):
        push_copy(k).start()

        @pl.when(k < nz // 2)
        def _():
            push_copy(nz - k).start()

    own_push = pltpu.make_async_copy(psend.at[z], serv.at[z], own_sem.at[2])
    own_push.start()
    stores = [
        pltpu.make_async_copy(src, dst, st_sem.at[i])
        for i, (src, dst) in enumerate(((m1v, m1_out), (m2v, m2_out), (mav, ma_out)))
    ]
    for store in stores:
        store.start()

    outputs = mm(hbuf[0].reshape(nz * cp, half), wv[0:half, :])
    outputs += mm(hbuf[1].reshape(nz * cp, half), wv[half:ff, :])
    product = outputs * rbuf[...].reshape(nz * cp, LANES).astype(F32)
    shares = mm(jnp.ones((8, LANES), F32), product, ((1,), (1,)), HIGHEST)
    for p in range(nz):
        ret_s[p, :, 0:cp] = shares[0:1, p * cp:(p + 1) * cp]

    def ret_copy(k):
        dest = lax.rem(z + k, nz)
        return remote(ret_s.at[place(dest)], ret_r.at[z], gs.at[k], gr.at[z], expert=dest)

    def ret_arrival(k):
        src = lax.rem(z + k, nz)
        return remote(ret_s.at[src], ret_r.at[src], gs.at[k], gr.at[src], expert=src)

    @pl.loop(1, nz // 2 + 1)
    def _(k):
        ret_copy(k).start()

        @pl.when(k < nz // 2)
        def _():
            ret_copy(nz - k).start()

    own_ret = pltpu.make_async_copy(ret_s.at[here], ret_r.at[z], own_sem.at[3])
    own_ret.start()
    own_ret.wait()

    @pl.loop(1, nz)
    def _(k):
        ret_arrival(k).wait_recv()

    for x in range(EXPERTS):
        total = ret_r[x * grp]
        for j in range(1, grp):
            total = total + ret_r[x * grp + j]
        cp_s[x:x + 1, :] = total

    def share_copy(k):
        return remote(cp_s, cp_r.at[k], ks.at[k], kr.at[k], copy=lax.rem(c + k, 4))

    for k in range(1, 4):
        share_copy(k).start()
    for k in range(1, 4):
        share_copy(k).wait_recv()
    whole = cp_s[...] + cp_r[1] + cp_r[2] + cp_r[3]
    whole = jnp.where(iota(whole.shape, 1) < cp, whole, 0.0)
    gate_grad = jnp.zeros((8, tok), F32)
    for x in range(EXPERTS):
        gate_grad += mm(jnp.broadcast_to(whole[x:x + 1], (8, LANES)), by_rank[x], precision=HIGHEST)
    logit_grad = (gate_grad[0:1] * gate) * (onehot - prob)
    gates[0:EXPERTS, :] = logit_grad
    grad_cols = gates[...].T
    term = inc[...].astype(F32)
    extra = grad_cols[:, 0:1] * rw_t[0:1, :]
    for x in range(1, EXPERTS):
        extra += grad_cols[:, x:x + 1] * rw_t[x:x + 1, :]
    ig_out[...] = (term + extra).astype(BF16)

    pend_copy.wait_send()
    for k in range(1, 4):
        share_copy(k).wait_send()

    @pl.when(b == e // 2)
    def _():
        for d in range(1, EXPERTS):
            first_copy(d).wait_send()

    @pl.loop(0, grp)
    def _(block):
        @pl.when((block <= m) & (m < grp - 1))
        def _():
            chain_copy(block, 0).wait_send()

        @pl.when((block >= m) & (m > 0))
        def _():
            chain_copy(block, 1).wait_send()

        x_copy(block, a).wait_send()
        core_copy(block, a, 0, b).wait_send()
        core_copy(block, 1 - a, 1, b).wait_send()

    @pl.loop(1, nz)
    def _(k):
        row_copy(k).wait_send()
        ret_copy(k).wait_send()

    for store in stores:
        store.wait()
    own_push.wait()

    @pl.loop(1, nz)
    def _(k):
        push_copy(k).wait_send()
        push_arrival(k).wait_recv()


def per_device(
    pending, hidden, logits, routes, router_weight, down_weight, master, moment_first, moment_second, push_plan,
):
    n_sec, nz = lax.axis_size("section"), lax.axis_size("expert")
    tok, width = pending.shape[1:]
    ff = hidden.shape[2]
    grp = nz // EXPERTS
    capacity = tok * 9 // (EXPERTS * 8)
    cp = 48
    gate_row = 40
    n_blocks = ff // PUSH_ROWS
    most = max(2, (3 * n_blocks + 2 * nz - 1) // (2 * nz))
    assert capacity <= gate_row and width == grp * LANES and tok == LANES
    per_owner = most * PUSH_ROWS
    half = ff // 2
    vmem, hbm = pl.BlockSpec(memory_space=pltpu.VMEM), pl.BlockSpec(memory_space=pl.ANY)
    dma = pltpu.SemaphoreType.DMA
    piece = jax.ShapeDtypeStruct((ff, LANES), F32)
    input_grad, fresh_master, first, second, serving = pl.pallas_call(
        functools.partial(kernel, n_sec, nz, cp, gate_row),
        out_shape=(
            jax.ShapeDtypeStruct((tok, width), BF16), piece, piece, piece,
            jax.ShapeDtypeStruct((nz, per_owner, LANES), BF16),
        ),
        in_specs=[hbm] + [vmem] * 4 + [hbm] * 4 + [vmem],
        out_specs=[vmem] + [hbm] * 4,
        scratch_shapes=[
            pltpu.VMEM((tok, width), BF16),
            pltpu.VMEM((2, EXPERTS, cp, half), BF16),
            pltpu.VMEM((2, 2, grp, 2, cp, half), BF16),
            pltpu.VMEM((nz, cp, LANES), BF16),
            pltpu.VMEM((nz, cp, LANES), BF16),
            pltpu.VMEM((nz, cp, LANES), BF16),
            pltpu.VMEM((LANES, LANES), F32),
            pltpu.VMEM((nz * per_owner, ff), BF16),
            pltpu.VMEM((nz, per_owner, LANES), BF16),
            pltpu.VMEM((nz, 1, LANES), F32),
            pltpu.VMEM((nz, 1, LANES), F32),
            pltpu.VMEM((EXPERTS, LANES), F32),
            pltpu.VMEM((4, EXPERTS, LANES), F32),
            pltpu.VMEM((ff, LANES), BF16),
            pltpu.VMEM((ff, LANES), F32),
            pltpu.VMEM((ff, LANES), F32),
            pltpu.VMEM((ff, LANES), F32),
            pltpu.VMEM((ff, LANES), BF16),
            dma((4,)), dma((3,)), dma((2,)), dma((4,)),
            dma((EXPERTS,)), dma((2,)),
            dma((2, grp)), dma((grp,)),
            dma((grp,)), dma((grp,)),
            dma((2, grp)), dma((2, grp)),
            dma((nz,)), dma((nz,)),
            dma((nz,)), dma((nz,)),
            dma((nz,)), dma((nz,)),
            dma((4,)), dma((4,)),
        ],
        compiler_params=pltpu.CompilerParams(
            collective_id=0, has_side_effects=True, vmem_limit_bytes=48 * 1024 * 1024
        ),
        cost_estimate=pl.CostEstimate(flops=10**9, bytes_accessed=8 * 10**6, transcendentals=10**5),
    )(
        pending[0], hidden[0], logits[0].T, routes[0].T, router_weight[0].T,
        down_weight[0, 0], master[0, 0], moment_first[0, 0], moment_second[0, 0], push_plan[0, 0, 0].T,
    )
    return (
        input_grad[None],
        fresh_master[None, None],
        first[None, None],
        second[None, None],
        serving.reshape(nz * most, PUSH_ROWS, LANES)[None, None, None],
    )


def solution(mesh):
    return jax.shard_map(
        per_device,
        mesh=mesh,
        in_specs=(
            P("section", "expert", "copy"),
            P("section", "expert", None),
            P("section", "expert", None),
            P("section", "expert", None),
            P("section", "copy", None),
            P("section", "copy", None, "expert"),
            P("section", "copy", None, "expert"),
            P("section", "copy", None, "expert"),
            P("section", "copy", None, "expert"),
            P("section", "copy", "expert", None, None),
        ),
        out_specs=(
            P("section", "expert", "copy"),
            P("section", "copy", None, "expert"),
            P("section", "copy", None, "expert"),
            P("section", "copy", None, "expert"),
            P("section", "copy", "expert", None, None, None),
        ),
        check_vma=False,
    )
```

time: 384 us -> 153 us (0.40)
  waiting for transfers between devices: 308 us -> 0 us
  Pallas kernels: 0 us -> 141 us
  starting transfers between devices: 47.7 us -> 0 us
  matrix products: 9.08 us -> 0 us
  local copies, waits for them, and re-layouts: 4.64 us -> 10.8 us
  blocking collectives: 5.66 us -> 0 us
  other arithmetic: 3.92 us -> 0 us
    all_to_all x5 -> x0, waiting for transfers between devices: 308 us -> none  [the longest x1 186 us: per_device(): lax.all_to_all(send_hidden, 'expert', split_axis=0, concat_axis=0, tiled=...]
    pallas_call x0 -> x1, Pallas kernels: none -> 141 us  [per_device(): pl.pallas_call(functools.partial(kernel, n_sec, nz, cp, gate_row), out_sh...]
    all_to_all x5 -> x0, starting transfers between devices: 44.9 us -> none  [the longest x1 28.7 us: per_device(): lax.all_to_all(send_gate, 'expert', split_axis=0, concat_axis=0, tiled=True)]
    unnamed x16 -> x25, local copies, waits for them, and re-layouts: 1.56 us -> 10.8 us
    dot_general x8 -> x0, matrix products: 9.08 us -> none  [the longest x1 3.24 us: per_device(): jnp.einsum('sif,sid->fd', hid_data, scaled, preferred_element_type=jnp.fl...]
    psum x1 -> x0, blocking collectives: 5.66 us -> none  [per_device(): gate_grad = lax.psum(gate_local, 'copy')]
  transfers between devices with their start and end apart: 6 -> 0, of which waited for: 5 -> 0; matrix products, arithmetic and copies ran while one was open for 4% -> 0% of each run, Pallas kernels for 0% -> 0%
where the time goes in v1:
time: 153 us; the launch traced here: 152 us
  Pallas kernels  141 us (92%)
  local copies, waits for them, and re-layouts  10.8 us (7%)
    pallas_call x1, Pallas kernels, per_device(): pl.pallas_call(functools.partial(kernel, n_sec, nz, cp, gate_row), out_sh...  141 us
    unnamed x25, local copies, waits for them, and re-layouts  10.8 us

profile of v1, /device:TPU:24, one launch (start us, length us, event | category | flops | bytes accessed | tf_op | source)
XLA Modules:
  0.0 152.0 jit_solution(2960753408241664057)
XLA Ops:
  0.6 0.0 copy-start.6
  0.6 0.0 copy-start.7
  0.7 0.0 copy-start.8
  0.7 0.7 copy-done.6
  1.4 0.0 copy-done.7
  1.4 0.0 copy-done.8
  1.4 0.0 copy-start
  1.4 1.0 copy-done
  2.4 0.0 copy-start.1
  2.4 1.0 copy-done.1
  3.4 0.0 copy-start.2
  3.4 1.0 copy-done.2
  4.3 0.0 copy-start.3
  4.4 0.9 copy-done.3
  5.3 0.0 copy-start.4
  5.3 0.9 copy-done.4
  6.2 0.0 copy-start.5
  6.2 0.9 copy-done.5
  7.2 0.0 copy-start.9
  7.2 0.7 copy-done.9
  7.8 140.5 %shard_map.137 = (bf16[128,1024]{1,0:T(8,128)(2,1)S(1)}, f32[768,128]{1,0:T(8,128)S(1)}, f32[768,128]{1,0:T(8,128)S(1)}, f32[768,128]{1,0:T(8,128)S(1)}, bf16[32,40,128]{2,1,0:T(8,128)(2,1)S(1)}) custom-call(bf16[128,1024]{1,0:T(8,128)(2,1)S(1)} %bitcast.27, bf16[128,768]{1,0:T(8,128)(2,1)S(1)} %bitcast.28, f32[4,128]{1,0:T(4,128)S(1)} %bitcast.31, ...), custom_call_target="tpu_custom_call" | custom-call | flops 1000000000 | bytes 8000000 | tf_op jit(solution)/shard_map/pallas_call | solution.py:411
  148.3 0.7 copy.20
  149.0 0.7 copy.21
  149.8 0.7 copy.22
  150.5 0.7 copy.23
  151.3 0.7 copy.24
Async XLA Ops:
  0.6 0.7 copy-start.6
  0.6 0.7 copy-start.7
  0.7 0.7 copy-start.8
  1.4 1.0 copy-start
  2.4 1.0 copy-start.1
  3.4 1.0 copy-start.2
  4.3 0.9 copy-start.3
  5.3 0.9 copy-start.4
  6.2 0.9 copy-start.5
  7.2 0.7 copy-start.9

commit v2 on v1

--- a/solution.py
+++ b/solution.py
@@ -37,7 +37,7 @@
     n_sec, nz, slot_rows, gate_row,
     pend, hid, log_t, route_t, rw_t, w_hbm, ma_hbm, m1_hbm, m2_hbm, plan,
     ig_out, ma_out, m1_out, m2_out, serv,
-    inc, hsend, hbuf, rsend, rbuf, scaled, gates, big, psend, ret_s, ret_r, cp_s, cp_r,
+    inc, hsend, hbuf, hflat, rsend, rbuf, scaled, gates, big, psend, ret_s, ret_r, cp_s, cp_r,
     wv, mav, m1v, m2v, fresh,
     ld_sem, st_sem, pend_sem, own_sem, ha_s, ha_r, zs, zr, xs, xr, cs, cr, rs, rr, ps, pr, gs, gr, ks, kr,
 ):
@@ -106,10 +106,10 @@
         rank_x = jnp.where(rid == x, rank, -1)
         by_rank.append((iota((LANES, tok), 0) == rank_x).astype(F32))
 
-    packed = mm(placing, hid[...]).astype(BF16)
+    packed = mm(placing, hid[...])
     for x in range(EXPERTS):
         for h in range(2):
-            hsend[h, x] = packed[x * cp:(x + 1) * cp, h * half:(h + 1) * half]
+            hsend[h, x] = packed[x * cp:(x + 1) * cp, h * half:(h + 1) * half].astype(BF16)
 
     def first_copy(d):
         other = lax.rem(e + d, EXPERTS)
@@ -129,11 +129,11 @@
     ]
 
     pend_copy.wait_recv()
+    rows = mm(placing, inc[...])
+    rid_rows = iota((cp, LANES), 0)
     for x in range(EXPERTS):
-        rows = mm(placing[x * cp:(x + 1) * cp], inc[...])
-        rid_rows = iota((cp, LANES), 0)
         for j in range(grp):
-            piece = rows[:, j * LANES:(j + 1) * LANES]
+            piece = rows[x * cp:(x + 1) * cp, j * LANES:(j + 1) * LANES]
             rsend[x * grp + j] = jnp.where(rid_rows >= gate_row, gate_rows[x], piece).astype(BF16)
 
     def row_copy(k):
@@ -144,13 +144,19 @@
         src = lax.rem(z + k, nz)
         return remote(rsend.at[src], rbuf.at[place(src)], rs.at[k], rr.at[place(src)], expert=src)
 
-    @pl.loop(1, nz // 2 + 1)
-    def _(k):
+    def row_pair(i):
+        k = nz // 2 - i
         row_copy(k).start()
 
         @pl.when(k < nz // 2)
         def _():
             row_copy(nz - k).start()
+
+    per_step = nz // 2 // grp
+
+    @pl.loop(0, per_step)
+    def _(i):
+        row_pair(i)
 
     own_rows = pltpu.make_async_copy(rsend.at[z], rbuf.at[here], own_sem.at[1])
     own_rows.start()
@@ -211,6 +217,9 @@
                 chain_copy(m + k, 1).start()
 
             spread(m + k)
+
+        for i in range(per_step):
+            row_pair(k * per_step + i)
 
     @pl.loop(0, grp)
     def _(block):
@@ -244,15 +253,19 @@
     def _(k):
         row_arrival(k).wait_recv()
 
+    def flat(blocks):
+        return blocks.astype(F32).reshape(nz * cp, blocks.shape[-1])
+
     gates[...] = jnp.zeros(gates.shape, F32)
     for p in range(nz):
-        gates[p:p + 1, :] = rbuf[p, 32:48, :].astype(F32)[gate_row - 32:gate_row - 31]
+        gates[p:p + 1, :] = rbuf[p].astype(F32)[gate_row:gate_row + 1]
     gate_cols = gates[...].T
     for p in range(nz):
-        scaled[p] = (gate_cols[0:cp, p:p + 1] * rbuf[p].astype(F32)).astype(BF16)
-    scaled_all = scaled[...].reshape(nz * cp, LANES)
+        scaled[p] = gate_cols[0:cp, p:p + 1] * rbuf[p].astype(F32)
+    scaled_all = scaled[...].reshape(nz * cp, LANES).astype(BF16)
     for h in range(2):
-        hidden_h = hbuf[h].reshape(nz * cp, half)
+        hidden_h = flat(hbuf[h]).astype(BF16)
+        hflat[h] = hidden_h
         grad = mm(scaled_all, hidden_h, ((0,), (0,))).T
         rows_h = pl.ds(h * half, half)
         first = beta_first * m1v[rows_h, :] + (1.0 - beta_first) * grad
@@ -263,6 +276,29 @@
         m2v[rows_h, :] = second
         mav[rows_h, :] = new
         fresh[rows_h, :] = new.astype(BF16)
+    outputs = mm(hflat[0], wv[0:half, :]) + mm(hflat[1], wv[half:ff, :])
+    product = outputs * flat(rbuf[...])
+    shares = mm(jnp.ones((8, LANES), F32), product, ((1,), (1,)), HIGHEST)
+    for p in range(nz):
+        ret_s[p, :, 0:cp] = shares[0:1, p * cp:(p + 1) * cp]
+
+    def ret_copy(k):
+        dest = lax.rem(z + k, nz)
+        return remote(ret_s.at[place(dest)], ret_r.at[z], gs.at[k], gr.at[z], expert=dest)
+
+    def ret_arrival(k):
+        src = lax.rem(z + k, nz)
+        return remote(ret_s.at[src], ret_r.at[src], gs.at[k], gr.at[src], expert=src)
+
+    @pl.loop(0, nz // 2)
+    def _(i):
+        k = nz // 2 - i
+        ret_copy(k).start()
+
+        @pl.when(k < nz // 2)
+        def _():
+            ret_copy(nz - k).start()
+
     per_owner = most * PUSH_ROWS
     for x in range(EXPERTS):
         part = mm(big[x * grp * per_owner:(x + 1) * grp * per_owner, :], fresh[...])
@@ -277,8 +313,9 @@
         src = lax.rem(z + k, nz)
         return remote(psend.at[src], serv.at[src], ps.at[k], pr.at[src], expert=src)
 
-    @pl.loop(1, nz // 2 + 1)
-    def _(k):
+    @pl.loop(0, nz // 2)
+    def _(i):
+        k = nz // 2 - i
         push_copy(k).start()
 
         @pl.when(k < nz // 2)
@@ -293,29 +330,6 @@
     ]
     for store in stores:
         store.start()
-
-    outputs = mm(hbuf[0].reshape(nz * cp, half), wv[0:half, :])
-    outputs += mm(hbuf[1].reshape(nz * cp, half), wv[half:ff, :])
-    product = outputs * rbuf[...].reshape(nz * cp, LANES).astype(F32)
-    shares = mm(jnp.ones((8, LANES), F32), product, ((1,), (1,)), HIGHEST)
-    for p in range(nz):
-        ret_s[p, :, 0:cp] = shares[0:1, p * cp:(p + 1) * cp]
-
-    def ret_copy(k):
-        dest = lax.rem(z + k, nz)
-        return remote(ret_s.at[place(dest)], ret_r.at[z], gs.at[k], gr.at[z], expert=dest)
-
-    def ret_arrival(k):
-        src = lax.rem(z + k, nz)
-        return remote(ret_s.at[src], ret_r.at[src], gs.at[k], gr.at[src], expert=src)
-
-    @pl.loop(1, nz // 2 + 1)
-    def _(k):
-        ret_copy(k).start()
-
-        @pl.when(k < nz // 2)
-        def _():
-            ret_copy(nz - k).start()
 
     own_ret = pltpu.make_async_copy(ret_s.at[here], ret_r.at[z], own_sem.at[3])
     own_ret.start()
@@ -398,8 +412,8 @@
     ff = hidden.shape[2]
     grp = nz // EXPERTS
     capacity = tok * 9 // (EXPERTS * 8)
-    cp = 48
-    gate_row = 40
+    cp = 40
+    gate_row = 36
     n_blocks = ff // PUSH_ROWS
     most = max(2, (3 * n_blocks + 2 * nz - 1) // (2 * nz))
     assert capacity <= gate_row and width == grp * LANES and tok == LANES
@@ -420,9 +434,10 @@
             pltpu.VMEM((tok, width), BF16),
             pltpu.VMEM((2, EXPERTS, cp, half), BF16),
             pltpu.VMEM((2, 2, grp, 2, cp, half), BF16),
+            pltpu.VMEM((2, nz * cp, half), BF16),
             pltpu.VMEM((nz, cp, LANES), BF16),
             pltpu.VMEM((nz, cp, LANES), BF16),
-            pltpu.VMEM((nz, cp, LANES), BF16),
+            pltpu.VMEM((nz, cp, LANES), F32),
             pltpu.VMEM((LANES, LANES), F32),
             pltpu.VMEM((nz * per_owner, ff), BF16),
             pltpu.VMEM((nz, per_owner, LANES), BF16),
@@ -446,7 +461,7 @@
             dma((4,)), dma((4,)),
         ],
         compiler_params=pltpu.CompilerParams(
-            collective_id=0, has_side_effects=True, vmem_limit_bytes=48 * 1024 * 1024
+            collective_id=0, has_side_effects=True, vmem_limit_bytes=63 * 1024 * 1024
         ),
         cost_estimate=pl.CostEstimate(flops=10**9, bytes_accessed=8 * 10**6, transcendentals=10**5),
     )(

time: 153 us -> 131 us (0.86)
  Pallas kernels: 141 us -> 124 us
  local copies, waits for them, and re-layouts: 10.8 us -> 5.83 us
    pallas_call x1, Pallas kernels: 141 us -> 124 us  [per_device(): pl.pallas_call(functools.partial(kernel, n_sec, nz, cp, gate_row), out_sh...]
    unnamed x25 -> x13, local copies, waits for them, and re-layouts: 10.8 us -> 5.83 us
where the time goes in v2:
time: 131 us
  Pallas kernels  124 us (95%)
  local copies, waits for them, and re-layouts  5.83 us (4%)
    pallas_call x1, Pallas kernels, per_device(): pl.pallas_call(functools.partial(kernel, n_sec, nz, cp, gate_row), out_sh...  124 us
    unnamed x13, local copies, waits for them, and re-layouts  5.83 us

profile of v2, /device:TPU:24, one launch (start us, length us, event | category | flops | bytes accessed | tf_op | source)
XLA Modules:
  0.0 130.8 jit_solution(2499987437220178884)
XLA Ops:
  0.6 124.3 %shard_map.137 = (bf16[128,1024]{1,0:T(8,128)(2,1)}, f32[768,128]{1,0:T(8,128)}, f32[768,128]{1,0:T(8,128)}, f32[768,128]{1,0:T(8,128)}, bf16[32,40,128]{2,1,0:T(8,128)(2,1)}) custom-call(bf16[128,1024]{1,0:T(8,128)(2,1)} %bitcast.27, bf16[128,768]{1,0:T(8,128)(2,1)} %bitcast.28, f32[4,128]{1,0:T(4,128)} %bitcast.31, s32[1,128]{1,0:T(1,128)} %bitcast.32, ...), custom_call_target="tpu_custom_call" | custom-call | flops 1000000000 | bytes 8000000 | tf_op jit(solution)/shard_map/pallas_call | solution.py:425
  125.0 0.0 copy-start.2
  125.0 1.7 %copy.20 = bf16[1,128,1024]{2,1,0:T(8,128)(2,1)} copy(bf16[1,128,1024]{2,1,0:T(8,128)(2,1)} %bitcast.23) | data formatting | bytes 524288
  126.7 0.0 copy-done.2
  126.7 0.0 copy-start.1
  126.7 0.7 copy.21
  127.4 0.4 copy-done.1
  127.8 0.0 copy-start
  127.8 0.7 copy.22
  128.6 0.4 copy-done
  129.0 0.0 copy-start.3
  129.0 0.7 copy.23
  129.7 0.4 copy-done.3
  130.1 0.7 copy.24
Async XLA Ops:
  125.0 1.7 %copy-start.2 = (f32[768,128]{1,0:T(8,128)S(1)}, f32[768,128]{1,0:T(8,128)}, u32[]{:S(2)}) copy-start(f32[768,128]{1,0:T(8,128)} %get-tuple-element.11) | copy-start | bytes 1179652
  126.7 1.1 copy-start.1
  127.8 1.1 copy-start
  129.0 1.1 copy-start.3

commit v3 on v2

--- a/solution.py
+++ b/solution.py
@@ -276,6 +276,34 @@
         m2v[rows_h, :] = second
         mav[rows_h, :] = new
         fresh[rows_h, :] = new.astype(BF16)
+    per_owner = most * PUSH_ROWS
+    for x in range(EXPERTS):
+        part = mm(big[x * grp * per_owner:(x + 1) * grp * per_owner, :], fresh[...])
+        for j in range(grp):
+            psend[x * grp + j] = part[j * per_owner:(j + 1) * per_owner].astype(BF16)
+
+    def push_copy(k):
+        dest = lax.rem(z + k, nz)
+        return remote(psend.at[dest], serv.at[z], ps.at[k], pr.at[z], expert=dest)
+
+    def push_arrival(k):
+        src = lax.rem(z + k, nz)
+        return remote(psend.at[src], serv.at[src], ps.at[k], pr.at[src], expert=src)
+
+    def push_pair(i):
+        k = nz // 2 - i
+        push_copy(k).start()
+
+        @pl.when(k < nz // 2)
+        def _():
+            push_copy(nz - k).start()
+
+    early = nz // 8
+
+    @pl.loop(0, early)
+    def _(i):
+        push_pair(i)
+
     outputs = mm(hflat[0], wv[0:half, :]) + mm(hflat[1], wv[half:ff, :])
     product = outputs * flat(rbuf[...])
     shares = mm(jnp.ones((8, LANES), F32), product, ((1,), (1,)), HIGHEST)
@@ -299,28 +327,9 @@
         def _():
             ret_copy(nz - k).start()
 
-    per_owner = most * PUSH_ROWS
-    for x in range(EXPERTS):
-        part = mm(big[x * grp * per_owner:(x + 1) * grp * per_owner, :], fresh[...])
-        for j in range(grp):
-            psend[x * grp + j] = part[j * per_owner:(j + 1) * per_owner].astype(BF16)
-
-    def push_copy(k):
-        dest = lax.rem(z + k, nz)
-        return remote(psend.at[dest], serv.at[z], ps.at[k], pr.at[z], expert=dest)
-
-    def push_arrival(k):
-        src = lax.rem(z + k, nz)
-        return remote(psend.at[src], serv.at[src], ps.at[k], pr.at[src], expert=src)
-
-    @pl.loop(0, nz // 2)
+    @pl.loop(early, nz // 2)
     def _(i):
-        k = nz // 2 - i
-        push_copy(k).start()
-
-        @pl.when(k < nz // 2)
-        def _():
-            push_copy(nz - k).start()
+        push_pair(i)
 
     own_push = pltpu.make_async_copy(psend.at[z], serv.at[z], own_sem.at[2])
     own_push.start()
@@ -364,7 +373,9 @@
     extra = grad_cols[:, 0:1] * rw_t[0:1, :]
     for x in range(1, EXPERTS):
         extra += grad_cols[:, x:x + 1] * rw_t[x:x + 1, :]
-    ig_out[...] = (term + extra).astype(BF16)
+    inc[...] = (term + extra).astype(BF16)
+    stores.append(pltpu.make_async_copy(inc, ig_out, st_sem.at[3]))
+    stores[3].start()
 
     pend_copy.wait_send()
     for k in range(1, 4):
@@ -402,6 +413,19 @@
     def _(k):
         push_copy(k).wait_send()
         push_arrival(k).wait_recv()
+
+
+def hand_over(n, *refs):
+    sources, dests, held, sems = refs[:n], refs[n:2 * n], refs[2 * n:3 * n], refs[3 * n]
+    fetches = [pltpu.make_async_copy(sources[i], held[i], sems.at[0, i]) for i in range(n)]
+    stores = [pltpu.make_async_copy(held[i], dests[i], sems.at[1, i]) for i in range(n)]
+    for fetch in fetches:
+        fetch.start()
+    for fetch, store in zip(fetches, stores):
+        fetch.wait()
+        store.start()
+    for store in stores:
+        store.wait()
 
 
 def per_device(
@@ -422,14 +446,14 @@
     vmem, hbm = pl.BlockSpec(memory_space=pltpu.VMEM), pl.BlockSpec(memory_space=pl.ANY)
     dma = pltpu.SemaphoreType.DMA
     piece = jax.ShapeDtypeStruct((ff, LANES), F32)
-    input_grad, fresh_master, first, second, serving = pl.pallas_call(
+    results = pl.pallas_call(
         functools.partial(kernel, n_sec, nz, cp, gate_row),
         out_shape=(
             jax.ShapeDtypeStruct((tok, width), BF16), piece, piece, piece,
             jax.ShapeDtypeStruct((nz, per_owner, LANES), BF16),
         ),
         in_specs=[hbm] + [vmem] * 4 + [hbm] * 4 + [vmem],
-        out_specs=[vmem] + [hbm] * 4,
+        out_specs=[hbm] * 5,
         scratch_shapes=[
             pltpu.VMEM((tok, width), BF16),
             pltpu.VMEM((2, EXPERTS, cp, half), BF16),
@@ -450,7 +474,7 @@
             pltpu.VMEM((ff, LANES), F32),
             pltpu.VMEM((ff, LANES), F32),
             pltpu.VMEM((ff, LANES), BF16),
-            dma((4,)), dma((3,)), dma((2,)), dma((4,)),
+            dma((4,)), dma((4,)), dma((2,)), dma((4,)),
             dma((EXPERTS,)), dma((2,)),
             dma((2, grp)), dma((grp,)),
             dma((grp,)), dma((grp,)),
@@ -468,6 +492,16 @@
         pending[0], hidden[0], logits[0].T, routes[0].T, router_weight[0].T,
         down_weight[0, 0], master[0, 0], moment_first[0, 0], moment_second[0, 0], push_plan[0, 0, 0].T,
     )
+    n = len(results)
+    input_grad, fresh_master, first, second, serving = pl.pallas_call(
+        functools.partial(hand_over, n),
+        out_shape=tuple(jax.ShapeDtypeStruct(r.shape, r.dtype) for r in results),
+        in_specs=[hbm] * n,
+        out_specs=[hbm] * n,
+        scratch_shapes=[pltpu.VMEM(r.shape, r.dtype) for r in results] + [dma((2, n))],
+        compiler_params=pltpu.CompilerParams(vmem_limit_bytes=63 * 1024 * 1024),
+        cost_estimate=pl.CostEstimate(flops=0, bytes_accessed=4 * 10**6, transcendentals=0),
+    )(*results)
     return (
         input_grad[None],
         fresh_master[None, None],

time: 131 us -> 126 us (0.962)
  local copies, waits for them, and re-layouts: 5.83 us -> 0 us
    unnamed x13 -> x0, local copies, waits for them, and re-layouts: 5.83 us -> none
    pallas_call x0 -> x1, Pallas kernels: none -> 2.28 us  [per_device(): pl.pallas_call(functools.partial(hand_over, n), out_shape=tuple((jax.Shap...]
    pallas_call x1, Pallas kernels: 124 us -> 122 us  [per_device(): pl.pallas_call(functools.partial(kernel, n_sec, nz, cp, gate_row), out_sh...]
where the time goes in v3:
time: 126 us; the launch traced here: 125 us
  Pallas kernels  125 us (99%)
    pallas_call x1, Pallas kernels, per_device(): pl.pallas_call(functools.partial(kernel, n_sec, nz, cp, gate_row), out_sh...  122 us

profile of v3, /device:TPU:24, one launch (start us, length us, event | category | flops | bytes accessed | tf_op | source)
XLA Modules:
  0.0 125.3 jit_solution(11019824558387249016)
XLA Ops:
  0.6 122.4 %shard_map.137 = (bf16[128,1024]{1,0:T(8,128)(2,1)}, f32[768,128]{1,0:T(8,128)}, f32[768,128]{1,0:T(8,128)}, f32[768,128]{1,0:T(8,128)}, bf16[32,40,128]{2,1,0:T(8,128)(2,1)}) custom-call(bf16[128,1024]{1,0:T(8,128)(2,1)} %bitcast.26, bf16[128,768]{1,0:T(8,128)(2,1)} %bitcast.28, f32[4,128]{1,0:T(4,128)} %bitcast.31, s32[1,128]{1,0:T(1,128)} %bitcast.32, ...), custom_call_target="tpu_custom_call" | custom-call | flops 1000000000 | bytes 8000000 | tf_op jit(solution)/shard_map/pallas_call | solution.py:449
  123.1 2.3 %shard_map.138 = (bf16[128,1024]{1,0:T(8,128)(2,1)}, f32[768,128]{1,0:T(8,128)}, f32[768,128]{1,0:T(8,128)}, f32[768,128]{1,0:T(8,128)}, bf16[32,40,128]{2,1,0:T(8,128)(2,1)}) custom-call(bf16[128,1024]{1,0:T(8,128)(2,1)} %get-tuple-element.15.refs_0_, f32[768,128]{1,0:T(8,128)} %get-tuple-element.16.refs_1_, f32[768,128]{1,0:T(8,128)} %get-tuple-element.17.refs_2_, ...), custom_call_target="tpu_custom_call" | custom-call | bytes 4000000 | tf_op jit(solution)/shard_map/pallas_call | solution.py:496

commit v4 on v3

--- a/solution.py
+++ b/solution.py
@@ -37,7 +37,7 @@
     n_sec, nz, slot_rows, gate_row,
     pend, hid, log_t, route_t, rw_t, w_hbm, ma_hbm, m1_hbm, m2_hbm, plan,
     ig_out, ma_out, m1_out, m2_out, serv,
-    inc, hsend, hbuf, hflat, rsend, rbuf, scaled, gates, big, psend, ret_s, ret_r, cp_s, cp_r,
+    inc, hsend, hbuf, hflat, outs, rsend, rbuf, scaled, gates, big, psend, ret_s, ret_r, cp_s, cp_r,
     wv, mav, m1v, m2v, fresh,
     ld_sem, st_sem, pend_sem, own_sem, ha_s, ha_r, zs, zr, xs, xr, cs, cr, rs, rr, ps, pr, gs, gr, ks, kr,
 ):
@@ -74,19 +74,19 @@
     def greet(**axis):
         pl.semaphore_signal(barrier, inc=1, device_id=axis, device_id_type=pl.DeviceIdType.MESH)
 
+    @pl.loop(0, nz // 2)
+    def _(i):
+        k = nz // 2 - i
+        greet(expert=lax.rem(z + k, nz))
+
+        @pl.when(k < nz // 2)
+        def _():
+            greet(expert=lax.rem(z + nz - k, nz))
+
     greet(section=prev_sec)
     greet(section=next_sec)
     for k in range(1, 4):
         greet(copy=lax.rem(c + k, 4))
-
-    @pl.loop(1, nz)
-    def _(k):
-        greet(expert=lax.rem(z + k, nz))
-
-    pl.semaphore_wait(barrier, nz - 1 + 3 + 2)
-
-    pend_copy = remote(pend, inc, pend_sem.at[0], pend_sem.at[1], section=prev_sec)
-    pend_copy.start()
 
     logit = log_t[...]
     expd = jnp.exp(logit - jnp.max(logit, axis=0, keepdims=True))
@@ -111,120 +111,9 @@
         for h in range(2):
             hsend[h, x] = packed[x * cp:(x + 1) * cp, h * half:(h + 1) * half].astype(BF16)
 
-    def first_copy(d):
-        other = lax.rem(e + d, EXPERTS)
-        return remote(hsend.at[a, other], hbuf.at[a, b, m, e % 2], ha_s.at[d], ha_r.at[e % 2],
-                      expert=other * grp + m)
-
-    own_hidden = pltpu.make_async_copy(hsend.at[a, e], hbuf.at[a, b, m, e % 2], own_sem.at[0])
-
-    @pl.when(b == e // 2)
-    def _():
-        for d in range(1, EXPERTS):
-            first_copy(d).start()
-        own_hidden.start()
-
     gate_rows = [
         mm(gate8, by_rank[x].astype(BF16), ((1,), (1,)))[0:1] for x in range(EXPERTS)
     ]
-
-    pend_copy.wait_recv()
-    rows = mm(placing, inc[...])
-    rid_rows = iota((cp, LANES), 0)
-    for x in range(EXPERTS):
-        for j in range(grp):
-            piece = rows[x * cp:(x + 1) * cp, j * LANES:(j + 1) * LANES]
-            rsend[x * grp + j] = jnp.where(rid_rows >= gate_row, gate_rows[x], piece).astype(BF16)
-
-    def row_copy(k):
-        dest = lax.rem(z + k, nz)
-        return remote(rsend.at[dest], rbuf.at[here], rs.at[k], rr.at[here], expert=dest)
-
-    def row_arrival(k):
-        src = lax.rem(z + k, nz)
-        return remote(rsend.at[src], rbuf.at[place(src)], rs.at[k], rr.at[place(src)], expert=src)
-
-    def row_pair(i):
-        k = nz // 2 - i
-        row_copy(k).start()
-
-        @pl.when(k < nz // 2)
-        def _():
-            row_copy(nz - k).start()
-
-    per_step = nz // 2 // grp
-
-    @pl.loop(0, per_step)
-    def _(i):
-        row_pair(i)
-
-    own_rows = pltpu.make_async_copy(rsend.at[z], rbuf.at[here], own_sem.at[1])
-    own_rows.start()
-
-    def chain_copy(block, way):
-        return remote(hbuf.at[a, b, block], hbuf.at[a, b, block], zs.at[way, block], zr.at[block],
-                      expert=lax.rem(z + (1 if way == 0 else nz - 1), nz))
-
-    def x_copy(block, h):
-        return remote(hbuf.at[h, b, block], hbuf.at[h, b, block], xs.at[block], xr.at[block],
-                      copy=(1 - a) * 2 + b)
-
-    def core_copy(block, h, kind, core):
-        return remote(hbuf.at[h, core, block], hbuf.at[h, core, block], cs.at[kind, block],
-                      cr.at[kind, block], copy=a * 2 + 1 - b)
-
-    for i in range(2):
-        @pl.when(2 * b + i != e)
-        def _():
-            remote(hsend.at[a, 0], hbuf.at[a, b, m, i], ha_s.at[0], ha_r.at[i], expert=m).wait_recv()
-
-    @pl.when(b == e // 2)
-    def _():
-        own_hidden.wait()
-
-    def spread(block):
-        x_copy(block, a).start()
-        core_copy(block, a, 0, b).start()
-
-    @pl.when(m < grp - 1)
-    def _():
-        chain_copy(m, 0).start()
-
-    @pl.when(m > 0)
-    def _():
-        chain_copy(m, 1).start()
-
-    spread(m)
-
-    @pl.loop(1, grp)
-    def _(k):
-        @pl.when(m - k >= 0)
-        def _():
-            chain_copy(m - k, 0).wait_recv()
-
-            @pl.when(m < grp - 1)
-            def _():
-                chain_copy(m - k, 0).start()
-
-            spread(m - k)
-
-        @pl.when(m + k < grp)
-        def _():
-            chain_copy(m + k, 1).wait_recv()
-
-            @pl.when(m > 0)
-            def _():
-                chain_copy(m + k, 1).start()
-
-            spread(m + k)
-
-        for i in range(per_step):
-            row_pair(k * per_step + i)
-
-    @pl.loop(0, grp)
-    def _(block):
-        x_copy(block, 1 - a).wait_recv()
-        core_copy(block, 1 - a, 1, b).start()
 
     n_blocks = plan.shape[1]
     most = psend.shape[1] // PUSH_ROWS
@@ -239,6 +128,122 @@
     key = key * PUSH_ROWS + iota((1, ff), 1) % PUSH_ROWS
     big[...] = (iota((nz * most * PUSH_ROWS, ff), 0) == key).astype(F32).astype(BF16)
 
+    pl.semaphore_wait(barrier, nz - 1 + 3 + 2)
+
+    pend_copy = remote(pend, inc, pend_sem.at[0], pend_sem.at[1], section=prev_sec)
+    pend_copy.start()
+
+    def first_copy(d):
+        other = lax.rem(e + d, EXPERTS)
+        return remote(hsend.at[a, other], hbuf.at[a, b, m, e % 2], ha_s.at[d], ha_r.at[e % 2],
+                      expert=other * grp + m)
+
+    own_hidden = pltpu.make_async_copy(hsend.at[a, e], hbuf.at[a, b, m, e % 2], own_sem.at[0])
+
+    @pl.when(b == e // 2)
+    def _():
+        for d in range(1, EXPERTS):
+            first_copy(d).start()
+        own_hidden.start()
+
+    pend_copy.wait_recv()
+    rows = mm(placing, inc[...])
+    rid_rows = iota((cp, LANES), 0)
+    for x in range(EXPERTS):
+        for j in range(grp):
+            piece = rows[x * cp:(x + 1) * cp, j * LANES:(j + 1) * LANES]
+            rsend[x * grp + j] = jnp.where(rid_rows >= gate_row, gate_rows[x], piece).astype(BF16)
+
+    def row_copy(k):
+        dest = lax.rem(z + k, nz)
+        return remote(rsend.at[dest], rbuf.at[here], rs.at[k], rr.at[here], expert=dest)
+
+    def row_arrival(k):
+        src = lax.rem(z + k, nz)
+        return remote(rsend.at[src], rbuf.at[place(src)], rs.at[k], rr.at[place(src)], expert=src)
+
+    def row_pair(i):
+        k = nz // 2 - i
+        row_copy(k).start()
+
+        @pl.when(k < nz // 2)
+        def _():
+            row_copy(nz - k).start()
+
+    per_step = nz // 2 // grp
+
+    @pl.loop(0, per_step)
+    def _(i):
+        row_pair(i)
+
+    own_rows = pltpu.make_async_copy(rsend.at[z], rbuf.at[here], own_sem.at[1])
+    own_rows.start()
+
+    def chain_copy(block, way):
+        return remote(hbuf.at[a, b, block], hbuf.at[a, b, block], zs.at[way, block], zr.at[block],
+                      expert=lax.rem(z + (1 if way == 0 else nz - 1), nz))
+
+    def x_copy(block, h):
+        return remote(hbuf.at[h, b, block], hbuf.at[h, b, block], xs.at[block], xr.at[block],
+                      copy=(1 - a) * 2 + b)
+
+    def core_copy(block, h, kind, core):
+        return remote(hbuf.at[h, core, block], hbuf.at[h, core, block], cs.at[kind, block],
+                      cr.at[kind, block], copy=a * 2 + 1 - b)
+
+    for i in range(2):
+        @pl.when(2 * b + i != e)
+        def _():
+            remote(hsend.at[a, 0], hbuf.at[a, b, m, i], ha_s.at[0], ha_r.at[i], expert=m).wait_recv()
+
+    @pl.when(b == e // 2)
+    def _():
+        own_hidden.wait()
+
+    def spread(block):
+        x_copy(block, a).start()
+        core_copy(block, a, 0, b).start()
+
+    @pl.when(m < grp - 1)
+    def _():
+        chain_copy(m, 0).start()
+
+    @pl.when(m > 0)
+    def _():
+        chain_copy(m, 1).start()
+
+    spread(m)
+
+    @pl.loop(1, grp)
+    def _(k):
+        @pl.when(m - k >= 0)
+        def _():
+            chain_copy(m - k, 0).wait_recv()
+
+            @pl.when(m < grp - 1)
+            def _():
+                chain_copy(m - k, 0).start()
+
+            spread(m - k)
+
+        @pl.when(m + k < grp)
+        def _():
+            chain_copy(m + k, 1).wait_recv()
+
+            @pl.when(m > 0)
+            def _():
+                chain_copy(m + k, 1).start()
+
+            spread(m + k)
+
+        for i in range(per_step):
+            row_pair(k * per_step + i)
+
+    @pl.loop(0, grp)
+    def _(block):
+        x_copy(block, 1 - a).wait_recv()
+        core_copy(block, 1 - a, 1, b).start()
+
     for load in loads:
         load.wait()
 
@@ -247,14 +252,18 @@
         core_copy(block, a, 0, 1 - b).wait_recv()
         core_copy(block, 1 - a, 1, 1 - b).wait_recv()
 
+    def flat(blocks):
+        return blocks.astype(F32).reshape(nz * cp, blocks.shape[-1])
+
+    for h in range(2):
+        hflat[h] = flat(hbuf[h]).astype(BF16)
+    outs[...] = mm(hflat[0], wv[0:half, :]) + mm(hflat[1], wv[half:ff, :])
+
     own_rows.wait()
 
     @pl.loop(1, nz)
     def _(k):
         row_arrival(k).wait_recv()
-
-    def flat(blocks):
-        return blocks.astype(F32).reshape(nz * cp, blocks.shape[-1])
 
     gates[...] = jnp.zeros(gates.shape, F32)
     for p in range(nz):
@@ -264,9 +273,7 @@
         scaled[p] = gate_cols[0:cp, p:p + 1] * rbuf[p].astype(F32)
     scaled_all = scaled[...].reshape(nz * cp, LANES).astype(BF16)
     for h in range(2):
-        hidden_h = flat(hbuf[h]).astype(BF16)
-        hflat[h] = hidden_h
-        grad = mm(scaled_all, hidden_h, ((0,), (0,))).T
+        grad = mm(scaled_all, hflat[h], ((0,), (0,))).T
         rows_h = pl.ds(h * half, half)
         first = beta_first * m1v[rows_h, :] + (1.0 - beta_first) * grad
         second = beta_second * m2v[rows_h, :] + (1.0 - beta_second) * grad * grad
@@ -304,8 +311,7 @@
     def _(i):
         push_pair(i)
 
-    outputs = mm(hflat[0], wv[0:half, :]) + mm(hflat[1], wv[half:ff, :])
-    product = outputs * flat(rbuf[...])
+    product = outs[...] * flat(rbuf[...])
     shares = mm(jnp.ones((8, LANES), F32), product, ((1,), (1,)), HIGHEST)
     for p in range(nz):
         ret_s[p, :, 0:cp] = shares[0:1, p * cp:(p + 1) * cp]
@@ -459,6 +465,7 @@
             pltpu.VMEM((2, EXPERTS, cp, half), BF16),
             pltpu.VMEM((2, 2, grp, 2, cp, half), BF16),
             pltpu.VMEM((2, nz * cp, half), BF16),
+            pltpu.VMEM((nz * cp, LANES), F32),
             pltpu.VMEM((nz, cp, LANES), BF16),
             pltpu.VMEM((nz, cp, LANES), BF16),
             pltpu.VMEM((nz, cp, LANES), F32),

time: 126 us -> 123 us (0.976)
  Pallas kernels: 125 us -> 123 us
    pallas_call x1, Pallas kernels: 122 us -> 120 us  [per_device(): pl.pallas_call(functools.partial(kernel, n_sec, nz, cp, gate_row), out_sh...]
where the time goes in v4:
time: 123 us
  Pallas kernels  123 us (100%)
    pallas_call x1, Pallas kernels, per_device(): pl.pallas_call(functools.partial(kernel, n_sec, nz, cp, gate_row), out_sh...  120 us

profile of v4, /device:TPU:24, one launch (start us, length us, event | category | flops | bytes accessed | tf_op | source)
XLA Modules:
  0.0 123.2 jit_solution(7845643343360152957)
XLA Ops:
  0.6 120.3 %shard_map.137 = (bf16[128,1024]{1,0:T(8,128)(2,1)}, f32[768,128]{1,0:T(8,128)}, f32[768,128]{1,0:T(8,128)}, f32[768,128]{1,0:T(8,128)}, bf16[32,40,128]{2,1,0:T(8,128)(2,1)}) custom-call(bf16[128,1024]{1,0:T(8,128)(2,1)} %bitcast.26, bf16[128,768]{1,0:T(8,128)(2,1)} %bitcast.28, f32[4,128]{1,0:T(4,128)} %bitcast.31, s32[1,128]{1,0:T(1,128)} %bitcast.32, ...), custom_call_target="tpu_custom_call" | custom-call | flops 1000000000 | bytes 8000000 | tf_op jit(solution)/shard_map/pallas_call | solution.py:455
  120.9 2.3 %shard_map.138 = (bf16[128,1024]{1,0:T(8,128)(2,1)}, f32[768,128]{1,0:T(8,128)}, f32[768,128]{1,0:T(8,128)}, f32[768,128]{1,0:T(8,128)}, bf16[32,40,128]{2,1,0:T(8,128)(2,1)}) custom-call(bf16[128,1024]{1,0:T(8,128)(2,1)} %get-tuple-element.15.refs_0_, f32[768,128]{1,0:T(8,128)} %get-tuple-element.16.refs_1_, f32[768,128]{1,0:T(8,128)} %get-tuple-element.17.refs_2_, ...), custom_call_target="tpu_custom_call" | custom-call | bytes 4000000 | tf_op jit(solution)/shard_map/pallas_call | solution.py:503

commit v5 on v4

--- a/solution.py
+++ b/solution.py
@@ -9,6 +9,7 @@
 
 PUSH_ROWS = 8
 EXPERTS = 4
+PARTS = 4
 LANES = 128
 
 beta_first = 0.9
@@ -423,8 +424,14 @@
 
 def hand_over(n, *refs):
     sources, dests, held, sems = refs[:n], refs[n:2 * n], refs[2 * n:3 * n], refs[3 * n]
-    fetches = [pltpu.make_async_copy(sources[i], held[i], sems.at[0, i]) for i in range(n)]
-    stores = [pltpu.make_async_copy(held[i], dests[i], sems.at[1, i]) for i in range(n)]
+    fetches, stores = [], []
+    for i in range(n):
+        rows = held[i].shape[0] // PARTS
+        for q in range(PARTS):
+            part = pl.ds(q * rows, rows)
+            k = i * PARTS + q
+            fetches.append(pltpu.make_async_copy(sources[i].at[part], held[i].at[part], sems.at[0, k]))
+            stores.append(pltpu.make_async_copy(held[i].at[part], dests[i].at[part], sems.at[1, k]))
     for fetch in fetches:
         fetch.start()
     for fetch, store in zip(fetches, stores):
@@ -505,7 +512,7 @@
         out_shape=tuple(jax.ShapeDtypeStruct(r.shape, r.dtype) for r in results),
         in_specs=[hbm] * n,
         out_specs=[hbm] * n,
-        scratch_shapes=[pltpu.VMEM(r.shape, r.dtype) for r in results] + [dma((2, n))],
+        scratch_shapes=[pltpu.VMEM(r.shape, r.dtype) for r in results] + [dma((2, n * PARTS))],
         compiler_params=pltpu.CompilerParams(vmem_limit_bytes=63 * 1024 * 1024),
         cost_estimate=pl.CostEstimate(flops=0, bytes_accessed=4 * 10**6, transcendentals=0),
     )(*results)

time: 123 us -> 124 us (level)
  no operation moved by 1% of the time
where the time goes in v5:
time: 124 us; the launch traced here: 123 us
  Pallas kernels  123 us (99%)
    pallas_call x1, Pallas kernels, per_device(): pl.pallas_call(functools.partial(kernel, n_sec, nz, cp, gate_row), out_sh...  120 us
    pallas_call x1, Pallas kernels, per_device(): pl.pallas_call(functools.partial(hand_over, n), out_shape=tuple((jax.Shap...  2.54 us

profile of v5, /device:TPU:24, one launch (start us, length us, event | category | flops | bytes accessed | tf_op | source)
XLA Modules:
  0.0 123.5 jit_solution(16346170640808004697)
XLA Ops:
  0.6 120.3 %shard_map.137 = (bf16[128,1024]{1,0:T(8,128)(2,1)}, f32[768,128]{1,0:T(8,128)}, f32[768,128]{1,0:T(8,128)}, f32[768,128]{1,0:T(8,128)}, bf16[32,40,128]{2,1,0:T(8,128)(2,1)}) custom-call(bf16[128,1024]{1,0:T(8,128)(2,1)} %bitcast.26, bf16[128,768]{1,0:T(8,128)(2,1)} %bitcast.28, f32[4,128]{1,0:T(4,128)} %bitcast.31, s32[1,128]{1,0:T(1,128)} %bitcast.32, ...), custom_call_target="tpu_custom_call" | custom-call | flops 1000000000 | bytes 8000000 | tf_op jit(solution)/shard_map/pallas_call | solution.py:462
  120.9 2.5 %shard_map.138 = (bf16[128,1024]{1,0:T(8,128)(2,1)}, f32[768,128]{1,0:T(8,128)}, f32[768,128]{1,0:T(8,128)}, f32[768,128]{1,0:T(8,128)}, bf16[32,40,128]{2,1,0:T(8,128)(2,1)}) custom-call(bf16[128,1024]{1,0:T(8,128)(2,1)} %get-tuple-element.15.refs_0_, f32[768,128]{1,0:T(8,128)} %get-tuple-element.16.refs_1_, f32[768,128]{1,0:T(8,128)} %get-tuple-element.17.refs_2_, ...), custom_call_target="tpu_custom_call" | custom-call | bytes 4000000 | tf_op jit(solution)/shard_map/pallas_call | solution.py:510
